TPU v7x, 32 devices: a whole 2x2x4 slice. The times are simulated.
32 devices in a mesh: src: 32 (over z, y, x, core), dst: 1.
Axes of the slice: x: 2, y: 2, z: 4, core: 2. Of those that a mesh axis runs over, the one named last changes fastest.
Arguments:
- out_density: float32 [16384], P('src'), may hold values from 0.008 to 0.08
- in_density: float32 [16384], P('dst'), may hold values from 0.008 to 0.08
- retention: float32 [16384], P('src'), may hold values from 0.15 to 0.75
- demand: float32 [16384], P('src'), may hold values from 0.5 to 4
- location: int32 [16384], replicated, may hold values from 0 to 16383
- scenario_blocks: int32 [32], replicated, may hold values from 0 to 127
Outputs:
- out_fitness: float32 [16384], P('src')
- in_fitness: float32 [16384], P('dst')
- levels: float32 [16384, 32], P('src', 'dst')
Inputs may be any that keep to these rules, and one draw needn't show every extreme that they name: `scenario_blocks`: scenario k extracts the 128 firms of block index b = scenario_blocks_k, firms 128 * b to 128 * b + 127. `location`: several firms may share a map cell, and some cells hold none.
All inputs are finite; a program needn't handle non-finite values.
Results may differ from a plain program's by a relative error of at most 0.0003.
Values sent between devices are 32-bit elements; how exact they have to be, the bound alone decides.
A program may use at most 64 MiB of HBM per device.

v0:
```python
import math
import jax
import jax.numpy as jnp
from jax import lax
from jax.sharding import PartitionSpec as P

SWEEPS = 2
ITERS = 2
EXTRACT = 128
MAP_SIDE = 256
RANGE = 18
far_weight = 0.015625


def on_device(out_density, in_density, retention, demand, location, scenario_blocks):
    rows_dev = out_density.shape[0]
    cols_dev = in_density.shape[0]
    firms = rows_dev * lax.axis_size("src")
    row_start = lax.axis_index("src") * rows_dev
    col_start = lax.axis_index("dst") * cols_dev
    height = math.gcd(rows_dev, 128)
    blocks = rows_dev // height
    col_ids = col_start + jnp.arange(cols_dev, dtype=jnp.int32)
    offsets = jnp.arange(blocks, dtype=jnp.int32) * height
    src_cells = lax.dynamic_slice_in_dim(location, row_start, rows_dev)
    dst_cells = lax.dynamic_slice_in_dim(location, col_start, cols_dev)
    src_row = src_cells // MAP_SIDE
    src_col = src_cells % MAP_SIDE
    dst_row = dst_cells // MAP_SIDE
    dst_col = dst_cells % MAP_SIDE
    out_fit = jnp.sqrt(out_density)
    in_fit = jnp.sqrt(in_density)

    def pair_weight(offset):
        row_ids = row_start + offset + jnp.arange(height, dtype=jnp.int32)
        row_gap = lax.dynamic_slice_in_dim(src_row, offset, height)[:, None] - dst_row[None, :]
        col_gap = lax.dynamic_slice_in_dim(src_col, offset, height)[:, None] - dst_col[None, :]
        nearby = row_gap * row_gap + col_gap * col_gap <= RANGE * RANGE
        affinity = jnp.where(nearby, 1.0, far_weight)
        return jnp.where(row_ids[:, None] != col_ids[None, :], affinity, 0.0)

    for sweep_no in range(SWEEPS):

        def row_part(offset):
            row_fit = lax.dynamic_slice_in_dim(out_fit, offset, height)
            weight = pair_weight(offset)
            ratios = weight * in_fit[None, :] / (1.0 + row_fit[:, None] * in_fit[None, :] * weight)
            return jnp.sum(ratios, axis=1)

        row_partial = lax.map(row_part, offsets).reshape(rows_dev)
        row_total = lax.psum(row_partial, "dst")
        out_fit = firms * out_density / row_total

        def col_part(running, offset):
            row_fit = lax.dynamic_slice_in_dim(out_fit, offset, height)
            weight = pair_weight(offset)
            ratios = weight * row_fit[:, None] / (1.0 + row_fit[:, None] * in_fit[None, :] * weight)
            return (running + jnp.sum(ratios, axis=0), None)

        col_partial, _ = lax.scan(col_part, jnp.zeros((cols_dev,), jnp.float32), offsets)
        col_total = lax.psum(col_partial, "src")
        in_fit = firms * in_density / col_total
    row_scale = retention / (firms * out_density)

    def coeff_block(offset):
        row_fit = lax.dynamic_slice_in_dim(out_fit, offset, height)
        scale_part = lax.dynamic_slice_in_dim(row_scale, offset, height)
        product = row_fit[:, None] * in_fit[None, :] * pair_weight(offset)
        chance = product / (1.0 + product)
        return chance * scale_part[:, None]

    coefficients = lax.map(coeff_block, offsets).reshape(rows_dev, cols_dev)
    scenarios = scenario_blocks.shape[0]
    portion = scenarios // lax.axis_size("dst")
    leading = lax.axis_index("dst") * portion
    firm_rows = row_start + jnp.arange(rows_dev, dtype=jnp.int32)
    retained = (firm_rows[:, None] // EXTRACT != scenario_blocks[None, :]).astype(jnp.float32)
    levels = retained * demand[:, None]
    for round_no in range(ITERS):
        every_row = lax.all_gather(levels, "src", axis=0, tiled=True)
        columns = lax.dynamic_slice_in_dim(every_row, col_start, cols_dev, 0)
        summed = lax.psum(
            jnp.dot(
                coefficients,
                columns,
                preferred_element_type=jnp.float32,
                precision=lax.Precision.HIGHEST,
            ),
            "dst",
        )
        levels = retained * (demand[:, None] + summed)
    result = lax.dynamic_slice_in_dim(levels, leading, portion, 1)
    return (out_fit, in_fit, result)


def solution(mesh):
    in_specs = (P("src"), P("dst"), P("src"), P("src"), P(), P())
    out_specs = (P("src"), P("dst"), P("src", "dst"))
    return jax.shard_map(
        on_device, mesh=mesh, in_specs=in_specs, out_specs=out_specs, check_vma=False
    )
```

profile of v0, /device:TPU:0, one launch (start us, length us, event | category | flops | bytes accessed | tf_op | source)
XLA Modules:
  0.0 580.2 jit_solution(1393125838560426272)
XLA Ops:
  7.3 0.9 add_select_fusion
  10.5 33.4 %while.55 = (s32[]{:T(128)}, f32[4,128]{1,0:T(4,128)S(1)}, s32[4]{0:T(128)S(1)}, s32[]{:T(128)}, s32[512]{0:T(512)S(1)}, /*index=5*/s32[16384]{0:T(1024)S(1)}, s...) while((s32[]{:T(128)}, f32[4,128]{1,0:T(4,128)S(1)}, ...), condition=%wide.region_2.3_spmd.clone, body=%wide.region_0.2_spmd.clone.sunk | while | flops 31457284 | bytes 203979 | solution.py:50
  13.9 4.9 fusion.33
  22.3 4.9 fusion.33
  30.6 4.9 fusion.33
  39.0 4.9 fusion.33
  44.6 34.3 %while.58 = (s32[]{:T(128)}, f32[16384]{0:T(1024)S(1)}, s32[4]{0:T(128)S(1)}, s32[]{:T(128)}, s32[512]{0:T(512)S(1)}, /*index=5*/s32[16384]{0:T(1024)S(1)}, s32[...) while((s32[]{:T(128)}, f32[16384]{0:T(1024)S(1)}, ...), condition=%wide.region_5.6_spmd.clone, body=%wide.region_3.5_spmd.clone.sunk | while | flops 31473796 | bytes 464593 | solution.py:60
  48.0 5.1 fusion.36
  56.6 5.1 fusion.36
  65.2 5.1 fusion.36
  73.8 5.1 fusion.36
  79.7 120.3 %all-reduce.3.cloned.1.call-done = f32[16384]{0:T(1024)} async-done(((f32[16384]{0:T(1024)}), f32[16384]{0:T(1024)}) %all-reduce.3.cloned.1.call-update) | async-done | bytes 65552 | tf_op jit(solution)/shard_map/psum | solution.py:61
  200.9 33.4 %while.56 = (s32[]{:T(128)}, f32[4,128]{1,0:T(4,128)S(1)}, s32[4]{0:T(128)S(1)}, s32[]{:T(128)}, s32[512]{0:T(512)S(1)}, /*index=5*/s32[16384]{0:T(1024)S(1)}, s...) while((s32[]{:T(128)}, f32[4,128]{1,0:T(4,128)S(1)}, ...), condition=%wide.region_9.10_spmd.clone, body=%wide.region_7.9_spmd.clone.sunk | while | flops 31457284 | bytes 203979 | solution.py:50
  204.3 4.9 fusion.34
  212.7 4.9 fusion.34
  221.0 4.9 fusion.34
  229.4 4.9 fusion.34
  235.0 34.3 %while.59 = (s32[]{:T(128)}, f32[16384]{0:T(1024)S(1)}, s32[4]{0:T(128)S(1)}, s32[]{:T(128)}, s32[512]{0:T(512)S(1)}, /*index=5*/s32[16384]{0:T(1024)S(1)}, s32[...) while((s32[]{:T(128)}, f32[16384]{0:T(1024)S(1)}, ...), condition=%wide.region_12.13_spmd.clone, body=%wide.region_10.12_spmd.clone.sunk | while | flops 31473796 | bytes 464593 | solution.py:60
  238.4 5.1 fusion.37
  247.0 5.1 fusion.37
  255.6 5.1 fusion.37
  264.2 5.1 fusion.37
  271.0 117.5 %all-reduce.5.cloned.1.call-done = f32[16384]{0:T(1024)} async-done(((f32[16384]{0:T(1024)}), f32[16384]{0:T(1024)}) %all-reduce.5.cloned.1.call-update) | async-done | bytes 65552 | tf_op jit(solution)/shard_map/psum | solution.py:61
  389.4 39.0 %while.57 = (s32[]{:T(128)}, f32[4,128,16384]{2,1,0:T(8,128)}, s32[4]{0:T(128)S(1)}, f32[512]{0:T(512)S(1)}, f32[16384]{0:T(1024)S(1)}, /*index=5*/s32[]{:T(128)...) while((s32[]{:T(128)}, f32[4,128,16384]{2,1,0:T(8,128)}, ...), condition=%wide.region_15.16_spmd.clone, body=%wide.region_14.15_spmd.clone.sunk | while | flops 29360260 | bytes 8593107 | solution.py:72
  392.9 6.3 %fusion.35 = f32[4,128,16384]{2,1,0:T(8,128)} fusion(f32[4,128,16384]{2,1,0:T(8,128)} %get-tuple-element.1026, s32[]{:T(128)} %get-tuple-element.1025, f32[128]{0:T(128)S(1)} %dynamic_slice.129, s32[16384]{0:T(1024)S(1)} %get-tuple-element.1048, s32[128]{0:T(128)S(1)} %dynamic_slice.130, s32[16384]{0:T(1024)S(1)} %get-tuple-element.1046, ...), kind=kLoop, calls=%fused_computation.17.clone.1 | loop fusion | flops 29360128 | bytes 8588288 | tf_op jit(solution)/shard_map/while/body/jit(dynamic_update_index_in_dim)/dynamic_update_slice | solution.py:72
  402.6 6.2 %fusion.35 = f32[4,128,16384]{2,1,0:T(8,128)} fusion(f32[4,128,16384]{2,1,0:T(8,128)} %get-tuple-element.1026, s32[]{:T(128)} %get-tuple-element.1025, f32[128]{0:T(128)S(1)} %dynamic_slice.129, s32[16384]{0:T(1024)S(1)} %get-tuple-element.1048, s32[128]{0:T(128)S(1)} %dynamic_slice.130, s32[16384]{0:T(1024)S(1)} %get-tuple-element.1046, ...), kind=kLoop, calls=%fused_computation.17.clone.1 | loop fusion | flops 29360128 | bytes 8588288 | tf_op jit(solution)/shard_map/while/body/jit(dynamic_update_index_in_dim)/dynamic_update_slice | solution.py:72
  412.4 6.3 %fusion.35 = f32[4,128,16384]{2,1,0:T(8,128)} fusion(f32[4,128,16384]{2,1,0:T(8,128)} %get-tuple-element.1026, s32[]{:T(128)} %get-tuple-element.1025, f32[128]{0:T(128)S(1)} %dynamic_slice.129, s32[16384]{0:T(1024)S(1)} %get-tuple-element.1048, s32[128]{0:T(128)S(1)} %dynamic_slice.130, s32[16384]{0:T(1024)S(1)} %get-tuple-element.1046, ...), kind=kLoop, calls=%fused_computation.17.clone.1 | loop fusion | flops 29360128 | bytes 8588288 | tf_op jit(solution)/shard_map/while/body/jit(dynamic_update_index_in_dim)/dynamic_update_slice | solution.py:72
  422.1 6.2 %fusion.35 = f32[4,128,16384]{2,1,0:T(8,128)} fusion(f32[4,128,16384]{2,1,0:T(8,128)} %get-tuple-element.1026, s32[]{:T(128)} %get-tuple-element.1025, f32[128]{0:T(128)S(1)} %dynamic_slice.129, s32[16384]{0:T(1024)S(1)} %get-tuple-element.1048, s32[128]{0:T(128)S(1)} %dynamic_slice.130, s32[16384]{0:T(1024)S(1)} %get-tuple-element.1046, ...), kind=kLoop, calls=%fused_computation.17.clone.1 | loop fusion | flops 29360128 | bytes 8588288 | tf_op jit(solution)/shard_map/while/body/jit(dynamic_update_index_in_dim)/dynamic_update_slice | solution.py:72
  428.3 20.0 %all-gather.3.cloned.1.call-done = f32[16384,32]{0,1:T(8,128)} async-done(((f32[512,32]{0,1:T(8,128)}), f32[16384,32]{0,1:T(8,128)}) %all-gather.3.cloned.1.call-update) | async-done | bytes 2097168 | tf_op jit(solution)/shard_map/all_gather | solution.py:80
  448.4 35.0 %fusion.17 = f32[512,32]{0,1:T(8,128)} fusion(f32[512,16384]{1,0:T(8,128)} %bitcast.30, f32[16384,32]{0,1:T(8,128)} %all-gather.3.cloned.1.call-done, f32[512]{0:T(512)S(1)} %copy-done.4, s32[512]{0:T(512)S(1)} %add_select_fusion.2, s32[32]{0:T(128)S(1)} %copy-done.5), kind=kOutput, calls=%fused_computation.36 | convolution fusion | flops 3221274624 | bytes 35721344 | tf_op jit(solution)/shard_map/dot_general | solution.py:83
  483.4 55.3 %all-gather.5.cloned.1.call-done = f32[16384,32]{0,1:T(8,128)} async-done(((f32[512,32]{0,1:T(8,128)}), f32[16384,32]{0,1:T(8,128)}) %all-gather.5.cloned.1.call-update) | async-done | bytes 2097168 | tf_op jit(solution)/shard_map/all_gather | solution.py:80
  538.7 35.0 %fusion.16 = f32[512,32]{0,1:T(8,128)} fusion(f32[512,16384]{1,0:T(8,128)} %bitcast.31, f32[16384,32]{0,1:T(8,128)} %all-gather.5.cloned.1.call-done, f32[512]{0:T(512)S(1)} %copy-done.4, s32[512]{0:T(512)S(1)} %add_select_fusion.2, s32[32]{0:T(128)S(1)} %copy-done.5), kind=kOutput, calls=%fused_computation.34 | convolution fusion | flops 3221274624 | bytes 35721344 | tf_op jit(solution)/shard_map/dot_general | solution.py:83
  (157 shorter events, 24.9 us)
Async XLA Ops:
  7.2 381.3 %copy-start.3 = (f32[16384]{0:T(1024)S(1)}, f32[16384]{0:T(1024)}, u32[]{:S(2)}) copy-start(f32[16384]{0:T(1024)} %param.17) | copy-start | bytes 196612
  7.2 262.9 %copy-start.4 = (f32[512]{0:T(512)S(1)}, f32[512]{0:T(512)}, u32[]{:S(2)}) copy-start(f32[512]{0:T(512)} %param.19) | copy-start | bytes 6148
  7.2 262.9 %copy-start.5 = (s32[32]{0:T(128)S(1)}, s32[32]{0:T(128)}, u32[]{:S(2)}) copy-start(s32[32]{0:T(128)} %param.21) | copy-start | bytes 388
  7.2 192.8 %all-reduce.3.cloned.1.call-start = ((), (), s32[]{:S(2)}) async-start(), calls=%async_computation | async-start | bytes 131072 | tf_op jit(solution)/shard_map/psum | solution.py:61
  78.9 0.6 copy-start.1
  79.6 308.9 %all-reduce.5.cloned.1.call-start = ((), (), s32[]{:S(2)}) async-start(), calls=%async_computation.1 | async-start | bytes 131072 | tf_op jit(solution)/shard_map/psum | solution.py:61
  269.4 0.6 copy-start.2
  270.0 178.4 %all-gather.3.cloned.1.call-start = ((), (), s32[]{:S(2)}) async-start(), calls=%async_computation.2 | async-start | bytes 2162688 | tf_op jit(solution)/shard_map/all_gather | solution.py:80
  270.8 267.9 %all-gather.5.cloned.1.call-start = ((), (), s32[]{:S(2)}) async-start(), calls=%async_computation.3 | async-start | bytes 2162688 | tf_op jit(solution)/shard_map/all_gather | solution.py:80
  428.3 55.1 %copy-start = (f32[16384]{0:T(1024)}, f32[16384]{0:T(1024)S(1)}, u32[]{:S(2)}) copy-start(f32[16384]{0:T(1024)S(1)} %get-tuple-element.1067) | copy-start | bytes 196612
  428.3 55.1 %copy-start.6 = (f32[512]{0:T(512)}, f32[512]{0:T(512)S(1)}, u32[]{:S(2)}) copy-start(f32[512]{0:T(512)S(1)} %get-tuple-element.1081) | copy-start | bytes 6148
Sparse Core Ops, SparseCore 0:
  79.7 120.2 all-reduce.2
  270.1 118.3 all-reduce.4
  391.4 56.9 all-gather.2
  483.5 55.1 all-gather.4
where the time goes:
time: 581 us; the launch traced here: 580 us
  waiting for transfers between devices  313 us (54%)
  other arithmetic  111 us (19%)
  matrix products  70 us (12%)
  loops' own time  52.4 us (9%)
  local copies, waits for them, and re-layouts  19.6 us (3%)
  between operations  13.9 us (2%)
    psum x2, waiting for transfers between devices, on_device(): col_total = lax.psum(col_partial, 'src')  238 us
    all_gather x2, waiting for transfers between devices, on_device(): every_row = lax.all_gather(levels, 'src', axis=0, tiled=True)  75.3 us
    dot_general x2, matrix products, on_device(): jnp.dot(coefficients, columns, preferred_element_type=jnp.float32, precis...  70 us
    reduce_sum x8, other arithmetic, col_part(): return (running + jnp.sum(ratios, axis=0), None)  40.9 us
    reduce_sum x8, other arithmetic, row_part(): return jnp.sum(ratios, axis=1)  39.1 us
    dynamic_update_slice x4, other arithmetic, on_device(): coefficients = lax.map(coeff_block, offsets).reshape(rows_dev, cols_dev)  25 us
    another operation x2, loops' own time, on_device(): lax.scan(col_part, jnp.zeros((cols_dev,), jnp.float32), offsets)  21.1 us
    another operation x2, loops' own time, on_device(): row_partial = lax.map(row_part, offsets).reshape(rows_dev)  20.9 us
  transfers between devices with their start and end apart: 4, of which 4 were waited for; matrix products, arithmetic and copies ran while one was open for 5% of the time, Pallas kernels for 0%

commit v1 on v0

--- a/solution.py
+++ b/solution.py
@@ -58,7 +58,11 @@
             return (running + jnp.sum(ratios, axis=0), None)
 
         col_partial, _ = lax.scan(col_part, jnp.zeros((cols_dev,), jnp.float32), offsets)
-        col_total = lax.psum(col_partial, "src")
+        col_total = col_partial
+        for hop in (1, 2, 4, 8, 16):
+            col_total = col_total + lax.ppermute(
+                col_total, "src", [(dev, dev ^ hop) for dev in range(32)]
+            )
         in_fit = firms * in_density / col_total
     row_scale = retention / (firms * out_density)
 

time: 581 us -> 373 us (0.64)
  waiting for transfers between devices: 313 us -> 91.2 us
  starting transfers between devices: 0.34 us -> 19.5 us
    psum x2 -> x0, waiting for transfers between devices: 238 us -> none  [on_device(): col_total = lax.psum(col_partial, 'src')]
    ppermute x0 -> x10, waiting for transfers between devices: none -> 22 us  [on_device(): lax.ppermute(col_total, 'src', [(dev, dev ^ hop) for dev in range(32)])]
    ppermute x0 -> x10, starting transfers between devices: none -> 19.2 us  [on_device(): lax.ppermute(col_total, 'src', [(dev, dev ^ hop) for dev in range(32)])]
    all_gather x2, waiting for transfers between devices: 75.3 us -> 69.1 us  [on_device(): every_row = lax.all_gather(levels, 'src', axis=0, tiled=True)]
  transfers between devices with their start and end apart: 4 -> 12, of which waited for: 4 -> 12; matrix products, arithmetic and copies ran while one was open for 5% -> 8% of each run, Pallas kernels for 0% -> 0%
where the time goes in v1:
time: 373 us; the launch traced here: 372 us
  other arithmetic  110 us (29%)
  waiting for transfers between devices  91.2 us (24%)
  matrix products  70 us (19%)
  loops' own time  48.8 us (13%)
  starting transfers between devices  19.5 us (5%)
  local copies, waits for them, and re-layouts  18.4 us (5%)
  between operations  14.2 us (4%)
    dot_general x2, matrix products, on_device(): jnp.dot(coefficients, columns, preferred_element_type=jnp.float32, precis...  70 us
    all_gather x2, waiting for transfers between devices, on_device(): every_row = lax.all_gather(levels, 'src', axis=0, tiled=True)  69.1 us
    reduce_sum x8, other arithmetic, col_part(): return (running + jnp.sum(ratios, axis=0), None)  40.8 us
    reduce_sum x8, other arithmetic, row_part(): return jnp.sum(ratios, axis=1)  39.1 us
    dynamic_update_slice x4, other arithmetic, on_device(): coefficients = lax.map(coeff_block, offsets).reshape(rows_dev, cols_dev)  25 us
    ppermute x10, waiting for transfers between devices, on_device(): lax.ppermute(col_total, 'src', [(dev, dev ^ hop) for dev in range(32)])  22 us
    another operation x2, loops' own time, on_device(): lax.scan(col_part, jnp.zeros((cols_dev,), jnp.float32), offsets)  21.1 us
    ppermute x10, starting transfers between devices, on_device(): lax.ppermute(col_total, 'src', [(dev, dev ^ hop) for dev in range(32)])  19.2 us
  transfers between devices with their start and end apart: 12, of which 12 were waited for; matrix products, arithmetic and copies ran while one was open for 8% of the time, Pallas kernels for 0%

profile of v1, /device:TPU:0, one launch (start us, length us, event | category | flops | bytes accessed | tf_op | source)
XLA Modules:
  0.0 371.8 jit_solution(18119418969427580277)
XLA Ops:
  10.5 31.7 %while.55 = (s32[]{:T(128)}, f32[4,128]{1,0:T(4,128)S(1)}, s32[4]{0:T(128)S(1)}, s32[]{:T(128)}, s32[512]{0:T(512)S(1)}, /*index=5*/s32[16384]{0:T(1024)S(1)}, s...) while((s32[]{:T(128)}, f32[4,128]{1,0:T(4,128)S(1)}, ...), condition=%wide.region_2.3_spmd.clone, body=%wide.region_0.2_spmd.clone.sunk | while | flops 31457284 | bytes 203979 | solution.py:50
  13.5 4.9 %fusion.33 = f32[128]{0:T(128)S(1)} fusion(f32[128]{0:T(128)S(1)} %dynamic_slice.121, f32[16384]{0:T(1024)S(1)} %get-tuple-element.889, s32[16384]{0:T(1024)S(1)} %get-tuple-element.888, s32[128]{0:T(128)S(1)} %dynamic_slice.122, s32[16384]{0:T(1024)S(1)} %get-tuple-element.886, s32[128]{0:T(128)S(1)} %dynamic_slice.123, s32[128]{0:T(128)S(1)} %iota_add_fusion.11), kind=kLoop, calls=%fused_computation.8.clone.1 | loop fusion | flops 31457152 | bytes 199168 | tf_op jit(solution)/shard_map/while/body/eval_jaxpr/reduce_sum | solution.py:48
  21.4 4.9 %fusion.33 = f32[128]{0:T(128)S(1)} fusion(f32[128]{0:T(128)S(1)} %dynamic_slice.121, f32[16384]{0:T(1024)S(1)} %get-tuple-element.889, s32[16384]{0:T(1024)S(1)} %get-tuple-element.888, s32[128]{0:T(128)S(1)} %dynamic_slice.122, s32[16384]{0:T(1024)S(1)} %get-tuple-element.886, s32[128]{0:T(128)S(1)} %dynamic_slice.123, s32[128]{0:T(128)S(1)} %iota_add_fusion.11), kind=kLoop, calls=%fused_computation.8.clone.1 | loop fusion | flops 31457152 | bytes 199168 | tf_op jit(solution)/shard_map/while/body/eval_jaxpr/reduce_sum | solution.py:48
  29.3 4.9 %fusion.33 = f32[128]{0:T(128)S(1)} fusion(f32[128]{0:T(128)S(1)} %dynamic_slice.121, f32[16384]{0:T(1024)S(1)} %get-tuple-element.889, s32[16384]{0:T(1024)S(1)} %get-tuple-element.888, s32[128]{0:T(128)S(1)} %dynamic_slice.122, s32[16384]{0:T(1024)S(1)} %get-tuple-element.886, s32[128]{0:T(128)S(1)} %dynamic_slice.123, s32[128]{0:T(128)S(1)} %iota_add_fusion.11), kind=kLoop, calls=%fused_computation.8.clone.1 | loop fusion | flops 31457152 | bytes 199168 | tf_op jit(solution)/shard_map/while/body/eval_jaxpr/reduce_sum | solution.py:48
  37.2 4.9 %fusion.33 = f32[128]{0:T(128)S(1)} fusion(f32[128]{0:T(128)S(1)} %dynamic_slice.121, f32[16384]{0:T(1024)S(1)} %get-tuple-element.889, s32[16384]{0:T(1024)S(1)} %get-tuple-element.888, s32[128]{0:T(128)S(1)} %dynamic_slice.122, s32[16384]{0:T(1024)S(1)} %get-tuple-element.886, s32[128]{0:T(128)S(1)} %dynamic_slice.123, s32[128]{0:T(128)S(1)} %iota_add_fusion.11), kind=kLoop, calls=%fused_computation.8.clone.1 | loop fusion | flops 31457152 | bytes 199168 | tf_op jit(solution)/shard_map/while/body/eval_jaxpr/reduce_sum | solution.py:48
  42.8 34.3 %while.58 = (s32[]{:T(128)}, f32[16384]{0:T(1024)S(1)}, s32[4]{0:T(128)S(1)}, s32[]{:T(128)}, s32[512]{0:T(512)S(1)}, /*index=5*/s32[16384]{0:T(1024)S(1)}, s32[...) while((s32[]{:T(128)}, f32[16384]{0:T(1024)S(1)}, ...), condition=%wide.region_5.6_spmd.clone, body=%wide.region_3.5_spmd.clone.sunk | while | flops 31473796 | bytes 464593 | solution.py:60
  46.3 5.1 %fusion.36 = f32[16384]{0:T(1024)S(1)} fusion(f32[16384]{0:T(1024)S(1)} %get-tuple-element.929, f32[128]{0:T(128)S(1)} %dynamic_slice.134, s32[16384]{0:T(1024)S(1)} %get-tuple-element.927, s32[128]{0:T(128)S(1)} %dynamic_slice.135, s32[16384]{0:T(1024)S(1)} %get-tuple-element.925, s32[128]{0:T(128)S(1)} %dynamic_slice.136, s32[128]{0:T(128)S(1)} %iota_add_fusion.14), kind=kLoop, calls=%fused_computation.24.clone.1 | loop fusion | flops 31440896 | bytes 264192 | tf_op jit(solution)/shard_map/while/body/eval_jaxpr/reduce_sum | solution.py:58
  54.8 5.1 %fusion.36 = f32[16384]{0:T(1024)S(1)} fusion(f32[16384]{0:T(1024)S(1)} %get-tuple-element.929, f32[128]{0:T(128)S(1)} %dynamic_slice.134, s32[16384]{0:T(1024)S(1)} %get-tuple-element.927, s32[128]{0:T(128)S(1)} %dynamic_slice.135, s32[16384]{0:T(1024)S(1)} %get-tuple-element.925, s32[128]{0:T(128)S(1)} %dynamic_slice.136, s32[128]{0:T(128)S(1)} %iota_add_fusion.14), kind=kLoop, calls=%fused_computation.24.clone.1 | loop fusion | flops 31440896 | bytes 264192 | tf_op jit(solution)/shard_map/while/body/eval_jaxpr/reduce_sum | solution.py:58
  63.4 5.1 %fusion.36 = f32[16384]{0:T(1024)S(1)} fusion(f32[16384]{0:T(1024)S(1)} %get-tuple-element.929, f32[128]{0:T(128)S(1)} %dynamic_slice.134, s32[16384]{0:T(1024)S(1)} %get-tuple-element.927, s32[128]{0:T(128)S(1)} %dynamic_slice.135, s32[16384]{0:T(1024)S(1)} %get-tuple-element.925, s32[128]{0:T(128)S(1)} %dynamic_slice.136, s32[128]{0:T(128)S(1)} %iota_add_fusion.14), kind=kLoop, calls=%fused_computation.24.clone.1 | loop fusion | flops 31440896 | bytes 264192 | tf_op jit(solution)/shard_map/while/body/eval_jaxpr/reduce_sum | solution.py:58
  72.0 5.1 %fusion.36 = f32[16384]{0:T(1024)S(1)} fusion(f32[16384]{0:T(1024)S(1)} %get-tuple-element.929, f32[128]{0:T(128)S(1)} %dynamic_slice.134, s32[16384]{0:T(1024)S(1)} %get-tuple-element.927, s32[128]{0:T(128)S(1)} %dynamic_slice.135, s32[16384]{0:T(1024)S(1)} %get-tuple-element.925, s32[128]{0:T(128)S(1)} %dynamic_slice.136, s32[128]{0:T(128)S(1)} %iota_add_fusion.14), kind=kLoop, calls=%fused_computation.24.clone.1 | loop fusion | flops 31440896 | bytes 264192 | tf_op jit(solution)/shard_map/while/body/eval_jaxpr/reduce_sum | solution.py:58
  92.6 3.7 collective-permute-start.4
  99.4 31.7 %while.56 = (s32[]{:T(128)}, f32[4,128]{1,0:T(4,128)S(1)}, s32[4]{0:T(128)S(1)}, s32[]{:T(128)}, s32[512]{0:T(512)S(1)}, /*index=5*/s32[16384]{0:T(1024)S(1)}, s...) while((s32[]{:T(128)}, f32[4,128]{1,0:T(4,128)S(1)}, ...), condition=%wide.region_8.9_spmd.clone, body=%wide.region_6.8_spmd.clone.sunk | while | flops 31457284 | bytes 203979 | solution.py:50
  102.4 4.9 %fusion.34 = f32[128]{0:T(128)S(1)} fusion(f32[128]{0:T(128)S(1)} %dynamic_slice.125, f32[16384]{0:T(1024)S(1)} %get-tuple-element.967, s32[16384]{0:T(1024)S(1)} %get-tuple-element.966, s32[128]{0:T(128)S(1)} %dynamic_slice.126, s32[16384]{0:T(1024)S(1)} %get-tuple-element.964, s32[128]{0:T(128)S(1)} %dynamic_slice.127, s32[128]{0:T(128)S(1)} %iota_add_fusion.12), kind=kLoop, calls=%fused_computation.13.clone.1 | loop fusion | flops 31457152 | bytes 199168 | tf_op jit(solution)/shard_map/while/body/eval_jaxpr/reduce_sum | solution.py:48
  110.3 4.9 %fusion.34 = f32[128]{0:T(128)S(1)} fusion(f32[128]{0:T(128)S(1)} %dynamic_slice.125, f32[16384]{0:T(1024)S(1)} %get-tuple-element.967, s32[16384]{0:T(1024)S(1)} %get-tuple-element.966, s32[128]{0:T(128)S(1)} %dynamic_slice.126, s32[16384]{0:T(1024)S(1)} %get-tuple-element.964, s32[128]{0:T(128)S(1)} %dynamic_slice.127, s32[128]{0:T(128)S(1)} %iota_add_fusion.12), kind=kLoop, calls=%fused_computation.13.clone.1 | loop fusion | flops 31457152 | bytes 199168 | tf_op jit(solution)/shard_map/while/body/eval_jaxpr/reduce_sum | solution.py:48
  118.2 4.9 %fusion.34 = f32[128]{0:T(128)S(1)} fusion(f32[128]{0:T(128)S(1)} %dynamic_slice.125, f32[16384]{0:T(1024)S(1)} %get-tuple-element.967, s32[16384]{0:T(1024)S(1)} %get-tuple-element.966, s32[128]{0:T(128)S(1)} %dynamic_slice.126, s32[16384]{0:T(1024)S(1)} %get-tuple-element.964, s32[128]{0:T(128)S(1)} %dynamic_slice.127, s32[128]{0:T(128)S(1)} %iota_add_fusion.12), kind=kLoop, calls=%fused_computation.13.clone.1 | loop fusion | flops 31457152 | bytes 199168 | tf_op jit(solution)/shard_map/while/body/eval_jaxpr/reduce_sum | solution.py:48
  126.1 4.9 %fusion.34 = f32[128]{0:T(128)S(1)} fusion(f32[128]{0:T(128)S(1)} %dynamic_slice.125, f32[16384]{0:T(1024)S(1)} %get-tuple-element.967, s32[16384]{0:T(1024)S(1)} %get-tuple-element.966, s32[128]{0:T(128)S(1)} %dynamic_slice.126, s32[16384]{0:T(1024)S(1)} %get-tuple-element.964, s32[128]{0:T(128)S(1)} %dynamic_slice.127, s32[128]{0:T(128)S(1)} %iota_add_fusion.12), kind=kLoop, calls=%fused_computation.13.clone.1 | loop fusion | flops 31457152 | bytes 199168 | tf_op jit(solution)/shard_map/while/body/eval_jaxpr/reduce_sum | solution.py:48
  131.8 34.3 %while.59 = (s32[]{:T(128)}, f32[16384]{0:T(1024)S(1)}, s32[4]{0:T(128)S(1)}, s32[]{:T(128)}, s32[512]{0:T(512)S(1)}, /*index=5*/s32[16384]{0:T(1024)S(1)}, s32[...) while((s32[]{:T(128)}, f32[16384]{0:T(1024)S(1)}, ...), condition=%wide.region_11.12_spmd.clone, body=%wide.region_9.11_spmd.clone.sunk | while | flops 31473796 | bytes 464593 | solution.py:60
  135.2 5.1 %fusion.37 = f32[16384]{0:T(1024)S(1)} fusion(f32[16384]{0:T(1024)S(1)} %get-tuple-element.1007, f32[128]{0:T(128)S(1)} %dynamic_slice.138, s32[16384]{0:T(1024)S(1)} %get-tuple-element.1005, s32[128]{0:T(128)S(1)} %dynamic_slice.139, s32[16384]{0:T(1024)S(1)} %get-tuple-element.1003, s32[128]{0:T(128)S(1)} %dynamic_slice.140, s32[128]{0:T(128)S(1)} %iota_add_fusion.15), kind=kLoop, calls=%fused_computation.30.clone.1 | loop fusion | flops 31440896 | bytes 264192 | tf_op jit(solution)/shard_map/while/body/eval_jaxpr/reduce_sum | solution.py:58
  143.8 5.1 %fusion.37 = f32[16384]{0:T(1024)S(1)} fusion(f32[16384]{0:T(1024)S(1)} %get-tuple-element.1007, f32[128]{0:T(128)S(1)} %dynamic_slice.138, s32[16384]{0:T(1024)S(1)} %get-tuple-element.1005, s32[128]{0:T(128)S(1)} %dynamic_slice.139, s32[16384]{0:T(1024)S(1)} %get-tuple-element.1003, s32[128]{0:T(128)S(1)} %dynamic_slice.140, s32[128]{0:T(128)S(1)} %iota_add_fusion.15), kind=kLoop, calls=%fused_computation.30.clone.1 | loop fusion | flops 31440896 | bytes 264192 | tf_op jit(solution)/shard_map/while/body/eval_jaxpr/reduce_sum | solution.py:58
  152.3 5.1 %fusion.37 = f32[16384]{0:T(1024)S(1)} fusion(f32[16384]{0:T(1024)S(1)} %get-tuple-element.1007, f32[128]{0:T(128)S(1)} %dynamic_slice.138, s32[16384]{0:T(1024)S(1)} %get-tuple-element.1005, s32[128]{0:T(128)S(1)} %dynamic_slice.139, s32[16384]{0:T(1024)S(1)} %get-tuple-element.1003, s32[128]{0:T(128)S(1)} %dynamic_slice.140, s32[128]{0:T(128)S(1)} %iota_add_fusion.15), kind=kLoop, calls=%fused_computation.30.clone.1 | loop fusion | flops 31440896 | bytes 264192 | tf_op jit(solution)/shard_map/while/body/eval_jaxpr/reduce_sum | solution.py:58
  160.9 5.1 %fusion.37 = f32[16384]{0:T(1024)S(1)} fusion(f32[16384]{0:T(1024)S(1)} %get-tuple-element.1007, f32[128]{0:T(128)S(1)} %dynamic_slice.138, s32[16384]{0:T(1024)S(1)} %get-tuple-element.1005, s32[128]{0:T(128)S(1)} %dynamic_slice.139, s32[16384]{0:T(1024)S(1)} %get-tuple-element.1003, s32[128]{0:T(128)S(1)} %dynamic_slice.140, s32[128]{0:T(128)S(1)} %iota_add_fusion.15), kind=kLoop, calls=%fused_computation.30.clone.1 | loop fusion | flops 31440896 | bytes 264192 | tf_op jit(solution)/shard_map/while/body/eval_jaxpr/reduce_sum | solution.py:58
  177.4 3.0 collective-permute-done.8
  180.4 3.6 collective-permute-start.9
  187.0 38.8 %while.57 = (s32[]{:T(128)}, f32[4,128,16384]{2,1,0:T(8,128)}, s32[4]{0:T(128)S(1)}, f32[512]{0:T(512)S(1)}, f32[16384]{0:T(1024)S(1)}, /*index=5*/s32[]{:T(128)...) while((s32[]{:T(128)}, f32[4,128,16384]{2,1,0:T(8,128)}, ...), condition=%wide.region_13.14_spmd.clone, body=%wide.region_12.13_spmd.clone.sunk | while | flops 29360260 | bytes 8593107 | solution.py:76
  190.5 6.3 %fusion.35 = f32[4,128,16384]{2,1,0:T(8,128)} fusion(f32[4,128,16384]{2,1,0:T(8,128)} %get-tuple-element.1026, s32[]{:T(128)} %get-tuple-element.1025, f32[128]{0:T(128)S(1)} %dynamic_slice.129, s32[16384]{0:T(1024)S(1)} %get-tuple-element.1048, s32[128]{0:T(128)S(1)} %dynamic_slice.130, s32[16384]{0:T(1024)S(1)} %get-tuple-element.1046, ...), kind=kLoop, calls=%fused_computation.17.clone.1 | loop fusion | flops 29360128 | bytes 8588288 | tf_op jit(solution)/shard_map/while/body/jit(dynamic_update_index_in_dim)/dynamic_update_slice | solution.py:76
  200.2 6.2 %fusion.35 = f32[4,128,16384]{2,1,0:T(8,128)} fusion(f32[4,128,16384]{2,1,0:T(8,128)} %get-tuple-element.1026, s32[]{:T(128)} %get-tuple-element.1025, f32[128]{0:T(128)S(1)} %dynamic_slice.129, s32[16384]{0:T(1024)S(1)} %get-tuple-element.1048, s32[128]{0:T(128)S(1)} %dynamic_slice.130, s32[16384]{0:T(1024)S(1)} %get-tuple-element.1046, ...), kind=kLoop, calls=%fused_computation.17.clone.1 | loop fusion | flops 29360128 | bytes 8588288 | tf_op jit(solution)/shard_map/while/body/jit(dynamic_update_index_in_dim)/dynamic_update_slice | solution.py:76
  209.9 6.3 %fusion.35 = f32[4,128,16384]{2,1,0:T(8,128)} fusion(f32[4,128,16384]{2,1,0:T(8,128)} %get-tuple-element.1026, s32[]{:T(128)} %get-tuple-element.1025, f32[128]{0:T(128)S(1)} %dynamic_slice.129, s32[16384]{0:T(1024)S(1)} %get-tuple-element.1048, s32[128]{0:T(128)S(1)} %dynamic_slice.130, s32[16384]{0:T(1024)S(1)} %get-tuple-element.1046, ...), kind=kLoop, calls=%fused_computation.17.clone.1 | loop fusion | flops 29360128 | bytes 8588288 | tf_op jit(solution)/shard_map/while/body/jit(dynamic_update_index_in_dim)/dynamic_update_slice | solution.py:76
  219.6 6.2 %fusion.35 = f32[4,128,16384]{2,1,0:T(8,128)} fusion(f32[4,128,16384]{2,1,0:T(8,128)} %get-tuple-element.1026, s32[]{:T(128)} %get-tuple-element.1025, f32[128]{0:T(128)S(1)} %dynamic_slice.129, s32[16384]{0:T(1024)S(1)} %get-tuple-element.1048, s32[128]{0:T(128)S(1)} %dynamic_slice.130, s32[16384]{0:T(1024)S(1)} %get-tuple-element.1046, ...), kind=kLoop, calls=%fused_computation.17.clone.1 | loop fusion | flops 29360128 | bytes 8588288 | tf_op jit(solution)/shard_map/while/body/jit(dynamic_update_index_in_dim)/dynamic_update_slice | solution.py:76
  225.8 13.8 %all-gather.3.cloned.1.call-done = f32[16384,32]{0,1:T(8,128)} async-done(((f32[512,32]{0,1:T(8,128)}), f32[16384,32]{0,1:T(8,128)}) %all-gather.3.cloned.1.call-update) | async-done | bytes 2097168 | tf_op jit(solution)/shard_map/all_gather | solution.py:84
  239.6 35.0 %fusion.17 = f32[512,32]{0,1:T(8,128)} fusion(f32[512,16384]{1,0:T(8,128)} %bitcast.30, f32[16384,32]{0,1:T(8,128)} %all-gather.3.cloned.1.call-done, f32[512]{0:T(512)S(1)} %copy-done.2, s32[512]{0:T(512)S(1)} %add_select_fusion.2, s32[32]{0:T(128)S(1)} %copy-done.3), kind=kOutput, calls=%fused_computation.36 | convolution fusion | flops 3221274624 | bytes 35721344 | tf_op jit(solution)/shard_map/dot_general | solution.py:87
  274.7 55.3 %all-gather.5.cloned.1.call-done = f32[16384,32]{0,1:T(8,128)} async-done(((f32[512,32]{0,1:T(8,128)}), f32[16384,32]{0,1:T(8,128)}) %all-gather.5.cloned.1.call-update) | async-done | bytes 2097168 | tf_op jit(solution)/shard_map/all_gather | solution.py:84
  330.0 35.0 %fusion.16 = f32[512,32]{0,1:T(8,128)} fusion(f32[512,16384]{1,0:T(8,128)} %bitcast.31, f32[16384,32]{0,1:T(8,128)} %all-gather.5.cloned.1.call-done, f32[512]{0:T(512)S(1)} %copy-done.2, s32[512]{0:T(512)S(1)} %add_select_fusion.2, s32[32]{0:T(128)S(1)} %copy-done.3), kind=kOutput, calls=%fused_computation.34 | convolution fusion | flops 3221274624 | bytes 35721344 | tf_op jit(solution)/shard_map/dot_general | solution.py:87
  (175 shorter events, 54.6 us)
Async XLA Ops:
  7.2 179.8 %copy-start.1 = (f32[16384]{0:T(1024)S(1)}, f32[16384]{0:T(1024)}, u32[]{:S(2)}) copy-start(f32[16384]{0:T(1024)} %param.17) | copy-start | bytes 196612
  7.2 176.9 %copy-start.2 = (f32[512]{0:T(512)S(1)}, f32[512]{0:T(512)}, u32[]{:S(2)}) copy-start(f32[512]{0:T(512)} %param.19) | copy-start | bytes 6148
  7.2 176.8 %copy-start.3 = (s32[32]{0:T(128)S(1)}, s32[32]{0:T(128)}, u32[]{:S(2)}) copy-start(s32[32]{0:T(128)} %param.21) | copy-start | bytes 388
  7.2 232.4 %all-gather.3.cloned.1.call-start = ((), (), s32[]{:S(2)}) async-start(), calls=%async_computation | async-start | bytes 2162688 | tf_op jit(solution)/shard_map/all_gather | solution.py:84
  77.1 1.4 collective-permute-start
  78.5 5.3 %collective-permute-start.1 = (f32[16384]{0:T(1024)S(1)}, f32[16384]{0:T(1024)S(1)}, u32[]{:S(2)}, u32[]{:S(2)}) collective-permute-start(f32[16384]{0:T(1024)S(1)} %add.246), channel_id=1, source_target_pairs={{0,2},{1,3},{2,0},{3,1},{4,6},{5,7},{6,4},{7,5},{8,10},{9,11},{10,... | collective-permute-start | bytes 196616 | tf_op jit(solution)/shard_map/ppermute | solution.py:63
  83.9 4.3 %collective-permute-start.2 = (f32[16384]{0:T(1024)S(1)}, f32[16384]{0:T(1024)S(1)}, u32[]{:S(2)}, u32[]{:S(2)}) collective-permute-start(f32[16384]{0:T(1024)S(1)} %add.247), channel_id=1, source_target_pairs={{0,4},{1,5},{2,6},{3,7},{4,0},{5,1},{6,2},{7,3},{8,12},{9,13},{10,... | collective-permute-start | bytes 196616 | tf_op jit(solution)/shard_map/ppermute | solution.py:63
  88.2 4.3 %collective-permute-start.3 = (f32[16384]{0:T(1024)S(1)}, f32[16384]{0:T(1024)S(1)}, u32[]{:S(2)}, u32[]{:S(2)}) collective-permute-start(f32[16384]{0:T(1024)S(1)} %add.248), channel_id=1, source_target_pairs={{0,8},{1,9},{2,10},{3,11},{4,12},{5,13},{6,14},{7,15},{8,0},{9,1},... | collective-permute-start | bytes 196616 | tf_op jit(solution)/shard_map/ppermute | solution.py:63
  92.6 5.9 %collective-permute-start.4 = (f32[16384]{0:T(1024)S(1)}, f32[16384]{0:T(1024)S(1)}, u32[]{:S(2)}, u32[]{:S(2)}) collective-permute-start(f32[16384]{0:T(1024)S(1)} %add.249), channel_id=1, source_target_pairs={{0,16},{1,17},{2,18},{3,19},{4,20},{5,21},{6,22},{7,23},{8,24},{9,... | collective-permute-start | bytes 196616 | tf_op jit(solution)/shard_map/ppermute | solution.py:63
  166.0 1.3 collective-permute-start.5
  167.4 4.3 %collective-permute-start.6 = (f32[16384]{0:T(1024)S(1)}, f32[16384]{0:T(1024)S(1)}, u32[]{:S(2)}, u32[]{:S(2)}) collective-permute-start(f32[16384]{0:T(1024)S(1)} %add.251), channel_id=1, source_target_pairs={{0,2},{1,3},{2,0},{3,1},{4,6},{5,7},{6,4},{7,5},{8,10},{9,11},{10,... | collective-permute-start | bytes 196616 | tf_op jit(solution)/shard_map/ppermute | solution.py:63
  171.7 4.3 %collective-permute-start.7 = (f32[16384]{0:T(1024)S(1)}, f32[16384]{0:T(1024)S(1)}, u32[]{:S(2)}, u32[]{:S(2)}) collective-permute-start(f32[16384]{0:T(1024)S(1)} %add.252), channel_id=1, source_target_pairs={{0,4},{1,5},{2,6},{3,7},{4,0},{5,1},{6,2},{7,3},{8,12},{9,13},{10,... | collective-permute-start | bytes 196616 | tf_op jit(solution)/shard_map/ppermute | solution.py:63
  176.1 4.3 %collective-permute-start.8 = (f32[16384]{0:T(1024)S(1)}, f32[16384]{0:T(1024)S(1)}, u32[]{:S(2)}, u32[]{:S(2)}) collective-permute-start(f32[16384]{0:T(1024)S(1)} %add.253), channel_id=1, source_target_pairs={{0,8},{1,9},{2,10},{3,11},{4,12},{5,13},{6,14},{7,15},{8,0},{9,1},... | collective-permute-start | bytes 196616 | tf_op jit(solution)/shard_map/ppermute | solution.py:63
  180.4 6.6 %collective-permute-start.9 = (f32[16384]{0:T(1024)S(1)}, f32[16384]{0:T(1024)S(1)}, u32[]{:S(2)}, u32[]{:S(2)}) collective-permute-start(f32[16384]{0:T(1024)S(1)} %add.254), channel_id=1, source_target_pairs={{0,16},{1,17},{2,18},{3,19},{4,20},{5,21},{6,22},{7,23},{8,24},{9,... | collective-permute-start | bytes 196616 | tf_op jit(solution)/shard_map/ppermute | solution.py:63
  184.8 145.2 %all-gather.5.cloned.1.call-start = ((), (), s32[]{:S(2)}) async-start(), calls=%async_computation.1 | async-start | bytes 2162688 | tf_op jit(solution)/shard_map/all_gather | solution.py:84
  225.8 48.8 %copy-start = (f32[16384]{0:T(1024)}, f32[16384]{0:T(1024)S(1)}, u32[]{:S(2)}) copy-start(f32[16384]{0:T(1024)S(1)} %get-tuple-element.1065) | copy-start | bytes 196612
  225.8 48.8 %copy-start.4 = (f32[512]{0:T(512)}, f32[512]{0:T(512)S(1)}, u32[]{:S(2)}) copy-start(f32[512]{0:T(512)S(1)} %get-tuple-element.1093) | copy-start | bytes 6148
Sparse Core Ops, SparseCore 0:
  184.9 54.7 all-gather.2
  274.8 55.1 all-gather.4
